TPU v7x, 32 devices: a whole 2x2x4 slice. The times are simulated.
32 devices in a mesh: groups: 2 (over x), srv: 16 (over z, y, core).
Axes of the slice: x: 2, y: 2, z: 4, core: 2. Of those that a mesh axis runs over, the one named last changes fastest.
Arguments:
- fields: bfloat16 [384, 336, 128], P(('groups', 'srv')), parts along dimension 0, may hold values from -6 to 6
- tile_count: int32 [192], P('srv'), may hold values from 32 to 128
- route: int32 [16, 16, 2], P('srv'), may hold values from 0 to 11, as said below
- weights: bfloat16 [9216, 128, 128], P('srv'), may hold values from -0.1875 to 0.1875
- block_src: int32 [9216], P('srv'), may hold values from 0 to 31, as said below
- destination_block: int32 [9216], P('srv'), may hold values from 0 to 255, as said below
- block_live: int32 [9216], P('srv'), may hold values from 0 to 1, as said below
Outputs:
- remapped: bfloat16 [512, 336, 128], P(('groups', 'srv')), parts along dimension 0
There are 2 independent parts, one for each index of `groups`. A program takes and returns all parts, laid end to end along the dimension named above; an argument that names none is the same for every part. Nothing has to cross between parts.
Inputs may be any that keep to these rules, and one draw needn't show every extreme that they name: route[s, d] lists 2 different blocks of compute rank d, as indices among its 12 blocks; every server needs exactly 2 blocks of every rank. block_src[k] = d * 2 + j names entry j of route[s, d] for the slot's server s = k // 576. `destination_block`: a slot of server s adds to one of the destination blocks (s * 16 + i) % 256 with 0 <= i <= 16: its own band or the first block of the next server's band. `block_live`: the live slots of each server come first among its 576 slots; some server has all of them live.
All inputs are finite; a program needn't handle non-finite values.
Results may differ from a plain program's by a relative error of at most 0.001.
Values may be sent and summed in bfloat16 or wider, within the bound.
A program may use at most 128 MiB of HBM per device.

v0:
```python
import jax
import jax.numpy as jnp
from jax import lax
from jax.sharding import PartitionSpec as P

DB_DEV = 16


slot_group = 32


def shifted(block, axis, distance):
    devices = range(lax.axis_size(axis))
    route = [((i - distance) % len(devices), i) for i in devices]
    return lax.ppermute(block, axis, route)


def shards(fields, tile_count, route, weights, block_src, destination_block, block_live):
    servers = lax.axis_size("srv")
    server = lax.axis_index("srv")
    held_blocks, row_count, block_width = fields.shape
    capacity = route.shape[2]
    positions = lax.broadcasted_iota(jnp.int32, (1, 1, block_width), 2)
    zero_value = jnp.zeros((), jnp.bfloat16)
    request_list = route[0]
    demanded = lax.all_to_all(request_list, "srv", split_axis=0, concat_axis=0, tiled=True)
    masked = jnp.where(positions < tile_count[:, None, None], fields, zero_value)
    outgoing = masked[demanded.reshape(-1)].reshape(servers, capacity, row_count, block_width)
    received = lax.all_to_all(outgoing, "srv", split_axis=0, concat_axis=0, tiled=True).reshape(
        servers * capacity, row_count, block_width
    )
    slot_count = weights.shape[0]
    groups = slot_count // slot_group
    local_rows = jnp.mod(destination_block - server * DB_DEV, DB_DEV * servers)
    living = block_live == 1

    def accumulate(totals, piece_set):
        w_group, source_group, rows_group, live_group = piece_set
        weighted_products = jnp.einsum(
            "krc,kdc->krd", received[source_group], w_group, preferred_element_type=jnp.float32
        )
        weighted_products = jnp.where(
            live_group[:, None, None], weighted_products, jnp.zeros((), jnp.float32)
        )
        return (totals.at[rows_group].add(weighted_products), None)

    start_totals = jnp.zeros((DB_DEV + 1, row_count, block_width), jnp.float32)
    totals, _ = lax.scan(
        accumulate,
        start_totals,
        (
            weights.reshape(groups, slot_group, block_width, block_width),
            block_src.reshape(groups, slot_group),
            local_rows.reshape(groups, slot_group),
            living.reshape(groups, slot_group),
        ),
    )
    excess_count = totals[DB_DEV]
    arrived = shifted(excess_count, "srv", 1)
    owned_rows = totals[:DB_DEV]
    owned_rows = owned_rows.at[0].add(arrived)
    return owned_rows.astype(jnp.bfloat16)


def solution(mesh):
    in_specs = (
        P(("groups", "srv"), None, None),
        P("srv"),
        P("srv", None, None),
        P("srv", None, None),
        P("srv"),
        P("srv"),
        P("srv"),
    )
    out_specs = P(("groups", "srv"), None, None)
    return jax.shard_map(shards, mesh=mesh, in_specs=in_specs, out_specs=out_specs, check_vma=False)
```

profile of v0, /device:TPU:7, one launch (start us, length us, event | category | flops | bytes accessed | tf_op | source)
XLA Modules:
  0.0 412.0 jit_solution(3859352883367652935)
XLA Ops:
  1.4 6.7 %all-to-all-start = ((s32[16,1,2]{2,1,0:T(1,128)}), s32[16,1,2]{2,1,0:T(1,128)S(1)}, u32[]{:S(2)}, u32[]{:S(2)}) async-start(s32[16,1,2]{2,1,0:T(1,128)} %copy.10), calls=%async_computation | async-start | bytes 16384 | tf_op jit(solution)/shard_map/all_to_all | solution.py:26
  22.1 55.2 %all-to-all-done.1 = bf16[16,2,336,128]{3,2,1,0:T(8,128)(2,1)S(1)} async-done(((bf16[16,2,336,128]{3,2,1,0:T(8,128)(2,1)}), bf16[16,2,336,128]{3,2,1,0:T(8,128)(2,1)S(1)}, u32[]{:S(2)}, u32[]{:S(2)}) %all-to-all-start.1) | async-done | bytes 2752544 | tf_op jit(solution)/shard_map/all_to_all | solution.py:29
  79.1 324.0 %while.11 = (s32[]{:T(128)}, f32[17,336,128]{2,1,0:T(8,128)S(1)}, s32[18,32]{1,0:T(8,128)S(1)}, pred[18,32]{1,0:T(8,128)(4,1)S(1)}, s32[18,32]{1,0:T(8,128)S(1)}...) while((s32[]{:T(128)}, f32[17,336,128]{2,1,0:T(8,128)S(1)}, ...), condition=%wide.region_2.3_spmd, body=%wide.region_0.2_spmd.sunk | while | flops 355075264 | bytes 31331400 | solution.py:48
  83.5 6.0 %broadcast_select_fusion.3 = f32[32,336,128]{2,1,0:T(8,128)} fusion(pred[32]{0:T(512)(128)(4,1)S(1)} %dynamic-slice_bitcast_fusion.2, bf16[32,336,128]{2,1,0:T(8,128)(2,1)} %gather_fusion, bf16[18,32,128,128]{3,2,1,0:T(8,128)(2,1)} %get-tuple-element.140, s32[]{:T(128)S(6)} %copy.14), kind=kOutput, calls=%fused_computation.3.clone.1 | convolution fusion | flops 353697792 | bytes 9306148 | tf_op jit(solution)/shard_map/while/body/eval_jaxpr/krc,kdc->krd/dot_general | solution.py:39
  89.5 7.6 %scatter_fusion = f32[17,336,128]{2,1,0:T(8,128)S(1)} fusion(f32[17,336,128]{2,1,0:T(8,128)S(1)} %get-tuple-element.127, s32[32]{0:T(128)S(1)} %get-tuple-element.116, f32[32,336,128]{2,1,0:T(8,128)} %broadcast_select_fusion.3), kind=kCustom, calls=%fused_computation.2.clone.1 | custom fusion | flops 1376256 | bytes 16515200 | tf_op jit(solution)/shard_map/while/body/eval_jaxpr/scatter-add | solution.py:45
  107.6 7.5 %scatter_fusion = f32[17,336,128]{2,1,0:T(8,128)S(1)} fusion(f32[17,336,128]{2,1,0:T(8,128)S(1)} %get-tuple-element.127, s32[32]{0:T(128)S(1)} %get-tuple-element.116, f32[32,336,128]{2,1,0:T(8,128)} %broadcast_select_fusion.3), kind=kCustom, calls=%fused_computation.2.clone.1 | custom fusion | flops 1376256 | bytes 16515200 | tf_op jit(solution)/shard_map/while/body/eval_jaxpr/scatter-add | solution.py:45
  125.5 7.6 %scatter_fusion = f32[17,336,128]{2,1,0:T(8,128)S(1)} fusion(f32[17,336,128]{2,1,0:T(8,128)S(1)} %get-tuple-element.127, s32[32]{0:T(128)S(1)} %get-tuple-element.116, f32[32,336,128]{2,1,0:T(8,128)} %broadcast_select_fusion.3), kind=kCustom, calls=%fused_computation.2.clone.1 | custom fusion | flops 1376256 | bytes 16515200 | tf_op jit(solution)/shard_map/while/body/eval_jaxpr/scatter-add | solution.py:45
  143.5 7.6 %scatter_fusion = f32[17,336,128]{2,1,0:T(8,128)S(1)} fusion(f32[17,336,128]{2,1,0:T(8,128)S(1)} %get-tuple-element.127, s32[32]{0:T(128)S(1)} %get-tuple-element.116, f32[32,336,128]{2,1,0:T(8,128)} %broadcast_select_fusion.3), kind=kCustom, calls=%fused_computation.2.clone.1 | custom fusion | flops 1376256 | bytes 16515200 | tf_op jit(solution)/shard_map/while/body/eval_jaxpr/scatter-add | solution.py:45
  155.5 6.0 %broadcast_select_fusion.3 = f32[32,336,128]{2,1,0:T(8,128)} fusion(pred[32]{0:T(512)(128)(4,1)S(1)} %dynamic-slice_bitcast_fusion.2, bf16[32,336,128]{2,1,0:T(8,128)(2,1)} %gather_fusion, bf16[18,32,128,128]{3,2,1,0:T(8,128)(2,1)} %get-tuple-element.140, s32[]{:T(128)S(6)} %copy.14), kind=kOutput, calls=%fused_computation.3.clone.1 | convolution fusion | flops 353697792 | bytes 9306148 | tf_op jit(solution)/shard_map/while/body/eval_jaxpr/krc,kdc->krd/dot_general | solution.py:39
  161.5 7.6 %scatter_fusion = f32[17,336,128]{2,1,0:T(8,128)S(1)} fusion(f32[17,336,128]{2,1,0:T(8,128)S(1)} %get-tuple-element.127, s32[32]{0:T(128)S(1)} %get-tuple-element.116, f32[32,336,128]{2,1,0:T(8,128)} %broadcast_select_fusion.3), kind=kCustom, calls=%fused_computation.2.clone.1 | custom fusion | flops 1376256 | bytes 16515200 | tf_op jit(solution)/shard_map/while/body/eval_jaxpr/scatter-add | solution.py:45
  173.5 6.0 %broadcast_select_fusion.3 = f32[32,336,128]{2,1,0:T(8,128)} fusion(pred[32]{0:T(512)(128)(4,1)S(1)} %dynamic-slice_bitcast_fusion.2, bf16[32,336,128]{2,1,0:T(8,128)(2,1)} %gather_fusion, bf16[18,32,128,128]{3,2,1,0:T(8,128)(2,1)} %get-tuple-element.140, s32[]{:T(128)S(6)} %copy.14), kind=kOutput, calls=%fused_computation.3.clone.1 | convolution fusion | flops 353697792 | bytes 9306148 | tf_op jit(solution)/shard_map/while/body/eval_jaxpr/krc,kdc->krd/dot_general | solution.py:39
  179.6 7.6 %scatter_fusion = f32[17,336,128]{2,1,0:T(8,128)S(1)} fusion(f32[17,336,128]{2,1,0:T(8,128)S(1)} %get-tuple-element.127, s32[32]{0:T(128)S(1)} %get-tuple-element.116, f32[32,336,128]{2,1,0:T(8,128)} %broadcast_select_fusion.3), kind=kCustom, calls=%fused_computation.2.clone.1 | custom fusion | flops 1376256 | bytes 16515200 | tf_op jit(solution)/shard_map/while/body/eval_jaxpr/scatter-add | solution.py:45
  191.5 6.0 %broadcast_select_fusion.3 = f32[32,336,128]{2,1,0:T(8,128)} fusion(pred[32]{0:T(512)(128)(4,1)S(1)} %dynamic-slice_bitcast_fusion.2, bf16[32,336,128]{2,1,0:T(8,128)(2,1)} %gather_fusion, bf16[18,32,128,128]{3,2,1,0:T(8,128)(2,1)} %get-tuple-element.140, s32[]{:T(128)S(6)} %copy.14), kind=kOutput, calls=%fused_computation.3.clone.1 | convolution fusion | flops 353697792 | bytes 9306148 | tf_op jit(solution)/shard_map/while/body/eval_jaxpr/krc,kdc->krd/dot_general | solution.py:39
  197.6 7.6 %scatter_fusion = f32[17,336,128]{2,1,0:T(8,128)S(1)} fusion(f32[17,336,128]{2,1,0:T(8,128)S(1)} %get-tuple-element.127, s32[32]{0:T(128)S(1)} %get-tuple-element.116, f32[32,336,128]{2,1,0:T(8,128)} %broadcast_select_fusion.3), kind=kCustom, calls=%fused_computation.2.clone.1 | custom fusion | flops 1376256 | bytes 16515200 | tf_op jit(solution)/shard_map/while/body/eval_jaxpr/scatter-add | solution.py:45
  209.5 6.0 %broadcast_select_fusion.3 = f32[32,336,128]{2,1,0:T(8,128)} fusion(pred[32]{0:T(512)(128)(4,1)S(1)} %dynamic-slice_bitcast_fusion.2, bf16[32,336,128]{2,1,0:T(8,128)(2,1)} %gather_fusion, bf16[18,32,128,128]{3,2,1,0:T(8,128)(2,1)} %get-tuple-element.140, s32[]{:T(128)S(6)} %copy.14), kind=kOutput, calls=%fused_computation.3.clone.1 | convolution fusion | flops 353697792 | bytes 9306148 | tf_op jit(solution)/shard_map/while/body/eval_jaxpr/krc,kdc->krd/dot_general | solution.py:39
  215.5 7.6 %scatter_fusion = f32[17,336,128]{2,1,0:T(8,128)S(1)} fusion(f32[17,336,128]{2,1,0:T(8,128)S(1)} %get-tuple-element.127, s32[32]{0:T(128)S(1)} %get-tuple-element.116, f32[32,336,128]{2,1,0:T(8,128)} %broadcast_select_fusion.3), kind=kCustom, calls=%fused_computation.2.clone.1 | custom fusion | flops 1376256 | bytes 16515200 | tf_op jit(solution)/shard_map/while/body/eval_jaxpr/scatter-add | solution.py:45
  227.5 6.0 %broadcast_select_fusion.3 = f32[32,336,128]{2,1,0:T(8,128)} fusion(pred[32]{0:T(512)(128)(4,1)S(1)} %dynamic-slice_bitcast_fusion.2, bf16[32,336,128]{2,1,0:T(8,128)(2,1)} %gather_fusion, bf16[18,32,128,128]{3,2,1,0:T(8,128)(2,1)} %get-tuple-element.140, s32[]{:T(128)S(6)} %copy.14), kind=kOutput, calls=%fused_computation.3.clone.1 | convolution fusion | flops 353697792 | bytes 9306148 | tf_op jit(solution)/shard_map/while/body/eval_jaxpr/krc,kdc->krd/dot_general | solution.py:39
  233.5 7.6 %scatter_fusion = f32[17,336,128]{2,1,0:T(8,128)S(1)} fusion(f32[17,336,128]{2,1,0:T(8,128)S(1)} %get-tuple-element.127, s32[32]{0:T(128)S(1)} %get-tuple-element.116, f32[32,336,128]{2,1,0:T(8,128)} %broadcast_select_fusion.3), kind=kCustom, calls=%fused_computation.2.clone.1 | custom fusion | flops 1376256 | bytes 16515200 | tf_op jit(solution)/shard_map/while/body/eval_jaxpr/scatter-add | solution.py:45
  251.5 7.6 %scatter_fusion = f32[17,336,128]{2,1,0:T(8,128)S(1)} fusion(f32[17,336,128]{2,1,0:T(8,128)S(1)} %get-tuple-element.127, s32[32]{0:T(128)S(1)} %get-tuple-element.116, f32[32,336,128]{2,1,0:T(8,128)} %broadcast_select_fusion.3), kind=kCustom, calls=%fused_computation.2.clone.1 | custom fusion | flops 1376256 | bytes 16515200 | tf_op jit(solution)/shard_map/while/body/eval_jaxpr/scatter-add | solution.py:45
  263.5 6.0 %broadcast_select_fusion.3 = f32[32,336,128]{2,1,0:T(8,128)} fusion(pred[32]{0:T(512)(128)(4,1)S(1)} %dynamic-slice_bitcast_fusion.2, bf16[32,336,128]{2,1,0:T(8,128)(2,1)} %gather_fusion, bf16[18,32,128,128]{3,2,1,0:T(8,128)(2,1)} %get-tuple-element.140, s32[]{:T(128)S(6)} %copy.14), kind=kOutput, calls=%fused_computation.3.clone.1 | convolution fusion | flops 353697792 | bytes 9306148 | tf_op jit(solution)/shard_map/while/body/eval_jaxpr/krc,kdc->krd/dot_general | solution.py:39
  269.5 7.6 %scatter_fusion = f32[17,336,128]{2,1,0:T(8,128)S(1)} fusion(f32[17,336,128]{2,1,0:T(8,128)S(1)} %get-tuple-element.127, s32[32]{0:T(128)S(1)} %get-tuple-element.116, f32[32,336,128]{2,1,0:T(8,128)} %broadcast_select_fusion.3), kind=kCustom, calls=%fused_computation.2.clone.1 | custom fusion | flops 1376256 | bytes 16515200 | tf_op jit(solution)/shard_map/while/body/eval_jaxpr/scatter-add | solution.py:45
  287.5 7.6 %scatter_fusion = f32[17,336,128]{2,1,0:T(8,128)S(1)} fusion(f32[17,336,128]{2,1,0:T(8,128)S(1)} %get-tuple-element.127, s32[32]{0:T(128)S(1)} %get-tuple-element.116, f32[32,336,128]{2,1,0:T(8,128)} %broadcast_select_fusion.3), kind=kCustom, calls=%fused_computation.2.clone.1 | custom fusion | flops 1376256 | bytes 16515200 | tf_op jit(solution)/shard_map/while/body/eval_jaxpr/scatter-add | solution.py:45
  305.5 7.6 %scatter_fusion = f32[17,336,128]{2,1,0:T(8,128)S(1)} fusion(f32[17,336,128]{2,1,0:T(8,128)S(1)} %get-tuple-element.127, s32[32]{0:T(128)S(1)} %get-tuple-element.116, f32[32,336,128]{2,1,0:T(8,128)} %broadcast_select_fusion.3), kind=kCustom, calls=%fused_computation.2.clone.1 | custom fusion | flops 1376256 | bytes 16515200 | tf_op jit(solution)/shard_map/while/body/eval_jaxpr/scatter-add | solution.py:45
  323.5 7.6 %scatter_fusion = f32[17,336,128]{2,1,0:T(8,128)S(1)} fusion(f32[17,336,128]{2,1,0:T(8,128)S(1)} %get-tuple-element.127, s32[32]{0:T(128)S(1)} %get-tuple-element.116, f32[32,336,128]{2,1,0:T(8,128)} %broadcast_select_fusion.3), kind=kCustom, calls=%fused_computation.2.clone.1 | custom fusion | flops 1376256 | bytes 16515200 | tf_op jit(solution)/shard_map/while/body/eval_jaxpr/scatter-add | solution.py:45
  335.5 6.0 %broadcast_select_fusion.3 = f32[32,336,128]{2,1,0:T(8,128)} fusion(pred[32]{0:T(512)(128)(4,1)S(1)} %dynamic-slice_bitcast_fusion.2, bf16[32,336,128]{2,1,0:T(8,128)(2,1)} %gather_fusion, bf16[18,32,128,128]{3,2,1,0:T(8,128)(2,1)} %get-tuple-element.140, s32[]{:T(128)S(6)} %copy.14), kind=kOutput, calls=%fused_computation.3.clone.1 | convolution fusion | flops 353697792 | bytes 9306148 | tf_op jit(solution)/shard_map/while/body/eval_jaxpr/krc,kdc->krd/dot_general | solution.py:39
  341.5 7.6 %scatter_fusion = f32[17,336,128]{2,1,0:T(8,128)S(1)} fusion(f32[17,336,128]{2,1,0:T(8,128)S(1)} %get-tuple-element.127, s32[32]{0:T(128)S(1)} %get-tuple-element.116, f32[32,336,128]{2,1,0:T(8,128)} %broadcast_select_fusion.3), kind=kCustom, calls=%fused_computation.2.clone.1 | custom fusion | flops 1376256 | bytes 16515200 | tf_op jit(solution)/shard_map/while/body/eval_jaxpr/scatter-add | solution.py:45
  353.5 6.0 %broadcast_select_fusion.3 = f32[32,336,128]{2,1,0:T(8,128)} fusion(pred[32]{0:T(512)(128)(4,1)S(1)} %dynamic-slice_bitcast_fusion.2, bf16[32,336,128]{2,1,0:T(8,128)(2,1)} %gather_fusion, bf16[18,32,128,128]{3,2,1,0:T(8,128)(2,1)} %get-tuple-element.140, s32[]{:T(128)S(6)} %copy.14), kind=kOutput, calls=%fused_computation.3.clone.1 | convolution fusion | flops 353697792 | bytes 9306148 | tf_op jit(solution)/shard_map/while/body/eval_jaxpr/krc,kdc->krd/dot_general | solution.py:39
  359.5 7.6 %scatter_fusion = f32[17,336,128]{2,1,0:T(8,128)S(1)} fusion(f32[17,336,128]{2,1,0:T(8,128)S(1)} %get-tuple-element.127, s32[32]{0:T(128)S(1)} %get-tuple-element.116, f32[32,336,128]{2,1,0:T(8,128)} %broadcast_select_fusion.3), kind=kCustom, calls=%fused_computation.2.clone.1 | custom fusion | flops 1376256 | bytes 16515200 | tf_op jit(solution)/shard_map/while/body/eval_jaxpr/scatter-add | solution.py:45
  371.5 6.0 %broadcast_select_fusion.3 = f32[32,336,128]{2,1,0:T(8,128)} fusion(pred[32]{0:T(512)(128)(4,1)S(1)} %dynamic-slice_bitcast_fusion.2, bf16[32,336,128]{2,1,0:T(8,128)(2,1)} %gather_fusion, bf16[18,32,128,128]{3,2,1,0:T(8,128)(2,1)} %get-tuple-element.140, s32[]{:T(128)S(6)} %copy.14), kind=kOutput, calls=%fused_computation.3.clone.1 | convolution fusion | flops 353697792 | bytes 9306148 | tf_op jit(solution)/shard_map/while/body/eval_jaxpr/krc,kdc->krd/dot_general | solution.py:39
  377.5 7.6 %scatter_fusion = f32[17,336,128]{2,1,0:T(8,128)S(1)} fusion(f32[17,336,128]{2,1,0:T(8,128)S(1)} %get-tuple-element.127, s32[32]{0:T(128)S(1)} %get-tuple-element.116, f32[32,336,128]{2,1,0:T(8,128)} %broadcast_select_fusion.3), kind=kCustom, calls=%fused_computation.2.clone.1 | custom fusion | flops 1376256 | bytes 16515200 | tf_op jit(solution)/shard_map/while/body/eval_jaxpr/scatter-add | solution.py:45
  389.5 6.0 %broadcast_select_fusion.3 = f32[32,336,128]{2,1,0:T(8,128)} fusion(pred[32]{0:T(512)(128)(4,1)S(1)} %dynamic-slice_bitcast_fusion.2, bf16[32,336,128]{2,1,0:T(8,128)(2,1)} %gather_fusion, bf16[18,32,128,128]{3,2,1,0:T(8,128)(2,1)} %get-tuple-element.140, s32[]{:T(128)S(6)} %copy.14), kind=kOutput, calls=%fused_computation.3.clone.1 | convolution fusion | flops 353697792 | bytes 9306148 | tf_op jit(solution)/shard_map/while/body/eval_jaxpr/krc,kdc->krd/dot_general | solution.py:39
  395.5 7.6 %scatter_fusion = f32[17,336,128]{2,1,0:T(8,128)S(1)} fusion(f32[17,336,128]{2,1,0:T(8,128)S(1)} %get-tuple-element.127, s32[32]{0:T(128)S(1)} %get-tuple-element.116, f32[32,336,128]{2,1,0:T(8,128)} %broadcast_select_fusion.3), kind=kCustom, calls=%fused_computation.2.clone.1 | custom fusion | flops 1376256 | bytes 16515200 | tf_op jit(solution)/shard_map/while/body/eval_jaxpr/scatter-add | solution.py:45
  (109 shorter events, 146.5 us)
Async XLA Ops:
  1.4 11.3 %all-to-all-start = ((s32[16,1,2]{2,1,0:T(1,128)}), s32[16,1,2]{2,1,0:T(1,128)S(1)}, u32[]{:S(2)}, u32[]{:S(2)}) async-start(s32[16,1,2]{2,1,0:T(1,128)} %copy.10), calls=%async_computation | async-start | bytes 16384 | tf_op jit(solution)/shard_map/all_to_all | solution.py:26
  16.4 5.5 %copy-start.1 = (s32[576]{0:T(1024)S(1)}, s32[576]{0:T(1024)}, u32[]{:S(2)}) copy-start(s32[576]{0:T(1024)} %param.17) | copy-start | bytes 6916
  16.4 5.6 %copy-start.2 = (s32[576]{0:T(1024)S(1)}, s32[576]{0:T(1024)}, u32[]{:S(2)}) copy-start(s32[576]{0:T(1024)} %param.16) | copy-start | bytes 6916
  16.4 5.7 %copy-start.3 = (s32[576]{0:T(1024)S(1)}, s32[576]{0:T(1024)}, u32[]{:S(2)}) copy-start(s32[576]{0:T(1024)} %param.15) | copy-start | bytes 6916
  16.4 61.0 %all-to-all-start.1 = ((bf16[16,2,336,128]{3,2,1,0:T(8,128)(2,1)}), bf16[16,2,336,128]{3,2,1,0:T(8,128)(2,1)S(1)}, u32[]{:S(2)}, u32[]{:S(2)}) async-start(bf16[16,2,336,128]{3,2,1,0:T(8,128)(2,1)} %bitcast.45), calls=%async_computation.1 | async-start | bytes 5505024 | tf_op jit(solution)/shard_map/all_to_all | solution.py:29
  77.4 1.5 copy-start
  403.1 8.2 %collective-permute-start = (f32[336,128]{1,0:T(8,128)S(1)}, f32[336,128]{1,0:T(8,128)S(1)}, u32[]{:S(2)}, u32[]{:S(2)}) collective-permute-start(f32[336,128]{1,0:T(8,128)S(1)} %slice_bitcast_fusion), channel_id=1, source_target_pairs={{15,0},{0,1},{1,2},{2,3},{3,4},{4,5},{5,6},{6,7},{7,8},{8,9},{9,10... | collective-permute-start | bytes 516104 | tf_op jit(solution)/shard_map/ppermute | solution.py:15
where the time goes:
time: 419 us; the launch traced here: 412 us
  other arithmetic  140 us (33%)
  matrix products  109 us (26%)
  local copies, waits for them, and re-layouts  85.5 us (20%)
  waiting for transfers between devices  58.9 us (14%)
  starting transfers between devices  18 us (4%)
    scatter-add x18, other arithmetic, accumulate(): return (totals.at[rows_group].add(weighted_products), None)  136 us
    dot_general x18, matrix products, accumulate(): jnp.einsum('krc,kdc->krd', received[source_group], w_group, preferred_ele...  109 us
    gather x18, local copies, waits for them, and re-layouts, accumulate(): received[source_group]  77.6 us
    all_to_all x1, waiting for transfers between devices, shards(): lax.all_to_all(outgoing, 'srv', split_axis=0, concat_axis=0, tiled=True)  55.2 us
  transfers between devices with their start and end apart: 3, of which 3 were waited for; matrix products, arithmetic and copies ran while one was open for 1% of the time, Pallas kernels for 0%

commit v1 on v0

v1 whole, which is shorter than its diff:
```python
import functools

import jax
import jax.numpy as jnp
from jax import lax
from jax.experimental import pallas as pl
from jax.experimental.pallas import tpu as pltpu
from jax.sharding import PartitionSpec as P

DB_DEV = 16
UNIT = 4
RING = 24


def plan(bucket, valid, n_buckets, source, steps_max):
    slots = bucket.shape[0]
    zero_source = -1
    ids = jnp.arange(n_buckets, dtype=jnp.int32)
    member = (bucket[None, :] == ids[:, None]) & valid[None, :]
    steps = (jnp.sum(member.astype(jnp.int32), axis=1) + UNIT - 1) // UNIT
    edges = jnp.arange(n_buckets + 1, dtype=jnp.int32)
    starts = jnp.sum(jnp.where(ids[None, :] < edges[:, None], steps[None, :], 0), axis=1)
    index = jnp.arange(slots, dtype=jnp.int32)
    before = jnp.sum(
        ((bucket[None, :] == bucket[:, None]) & valid[None, :] & (index[None, :] < index[:, None])).astype(jnp.int32),
        axis=1,
    )
    own = jnp.sum(jnp.where(ids[None, :] < bucket[:, None], steps[None, :], 0), axis=1)
    place = jnp.where(valid, own * UNIT + before, -1)
    places = jnp.arange(steps_max * UNIT, dtype=jnp.int32)
    hit = places[:, None] == place[None, :]
    slot = jnp.sum(jnp.where(hit, index[None, :], 0), axis=1)
    src = jnp.sum(jnp.where(hit, source[None, :] - zero_source, 0), axis=1) + zero_source
    return starts, slot, src


def product_kernel(first, last, finish, starts, slot, src, x_hbm, w_hbm, *refs):
    if finish is None:
        out, x, ring, x_sem, w_sem = refs
        prev = None
    else:
        prev, *refs = refs
        *outs, x, ring, acc, x_sem, w_sem = refs
    blocks = x_hbm.shape[0]
    load = pltpu.make_async_copy(x_hbm, x.at[pl.ds(0, blocks)], x_sem)
    load.start()
    begin, end = starts[first], starts[last]

    def fetch(p):
        for u in range(UNIT):
            pltpu.make_async_copy(
                w_hbm.at[slot[p * UNIT + u]], ring.at[lax.rem(p, RING), u], w_sem.at[lax.rem(p, RING)]
            ).start()

    def prime(p, carry):
        fetch(p)
        return carry

    lax.fori_loop(begin, jnp.minimum(end, begin + RING), prime, 0)
    x[blocks] = jnp.zeros(x.shape[1:], x.dtype)
    load.wait()

    def step(total, p, carry):
        at = lax.rem(p, RING)
        pltpu.make_async_copy(ring.at[at], ring.at[at], w_sem.at[at]).wait()
        lhs = jnp.concatenate([x[jnp.where(src[p * UNIT + u] < 0, blocks, src[p * UNIT + u])] for u in range(UNIT)], axis=1)
        rhs = jnp.concatenate([ring[at, u] for u in range(UNIT)], axis=1)
        total[...] += lax.dot_general(lhs, rhs, (((1,), (1,)), ((), ())), preferred_element_type=jnp.float32)

        @pl.when(p + RING < end)
        def _():
            fetch(p + RING)

        return carry

    def bucket(b, carry):
        if finish is None:
            total = out.at[b - first]
            total[...] = jnp.zeros(total.shape, total.dtype)
        else:
            total = acc
            total[...] = prev[b - first]
        lax.fori_loop(starts[b], starts[b + 1], functools.partial(step, total), 0)
        if finish is not None:
            finish(b - first, total, outs)
        return carry

    lax.fori_loop(first, last, bucket, 0)


def products(starts, slot, src, x, w, first, last, prev=None, finish=None, out_shape=None):
    blocks, rows, width = x.shape
    if finish is None:
        out_shape = jax.ShapeDtypeStruct((last - first, rows, width), jnp.float32)
        acc = []
    else:
        acc = [pltpu.VMEM((rows, width), jnp.float32)]
    smem = pl.BlockSpec(memory_space=pltpu.SMEM)
    hbm = pl.BlockSpec(memory_space=pl.ANY)
    vmem = pl.BlockSpec(memory_space=pltpu.VMEM)
    ins = [starts, slot, src, x, w] + ([] if prev is None else [prev])
    n_slots = w.shape[0] * (last - first) // 34
    return pl.pallas_call(
        functools.partial(product_kernel, first, last, finish),
        out_shape=out_shape,
        in_specs=[smem] * 3 + [hbm] * 2 + ([] if prev is None else [vmem]),
        out_specs=jax.tree.map(lambda _: vmem, out_shape),
        scratch_shapes=[
            pltpu.VMEM((blocks + 1, rows, width), x.dtype),
            pltpu.VMEM((RING, UNIT, width, width), w.dtype),
            *acc,
            pltpu.SemaphoreType.DMA,
            pltpu.SemaphoreType.DMA((RING,)),
        ],
        compiler_params=pltpu.CompilerParams(vmem_limit_bytes=24 << 20),
        cost_estimate=pl.CostEstimate(
            flops=4 * n_slots * rows * width * width, bytes_accessed=4 * n_slots * width * width, transcendentals=0
        ),
    )(*ins)


def select_kernel(demanded, tile_count, fields, *outs):
    servers = outs[0].shape[0]
    rows, width = fields.shape[1:]
    cells = lax.broadcasted_iota(jnp.int32, (rows, width), 1)

    def serve(s, carry):
        for j, out in enumerate(outs):
            block = demanded[s * len(outs) + j]
            kept = jnp.where(cells < tile_count[block], fields[block].astype(jnp.float32), 0.0)
            out[s] = kept.astype(fields.dtype)
        return carry

    lax.fori_loop(0, servers, serve, 0)


def select(demanded, tile_count, fields):
    servers, capacity = demanded.shape
    smem = pl.BlockSpec(memory_space=pltpu.SMEM)
    vmem = pl.BlockSpec(memory_space=pltpu.VMEM)
    return pl.pallas_call(
        select_kernel,
        out_shape=[jax.ShapeDtypeStruct((servers, *fields.shape[1:]), fields.dtype)] * capacity,
        in_specs=[smem, smem, vmem],
        out_specs=[vmem] * capacity,
        compiler_params=pltpu.CompilerParams(vmem_limit_bytes=24 << 20),
    )(demanded.reshape(-1), tile_count, fields)


def finish_rows(i, total, outs):
    out, head = outs

    @pl.when(i == 0)
    def _():
        head[...] = total[...]

    out[i] = total[...].astype(out.dtype)


def finish_excess(i, total, outs):
    outs[0][...] = total[...]


def shards(fields, tile_count, route, weights, block_src, destination_block, block_live):
    servers = lax.axis_size("srv")
    server = lax.axis_index("srv")
    held, rows, width = fields.shape
    slots = weights.shape[0]
    capacity = route.shape[2]
    band = DB_DEV
    demanded = lax.all_to_all(route[0], "srv", split_axis=0, concat_axis=0, tiled=True)
    received = [
        lax.all_to_all(part, "srv", split_axis=0, concat_axis=0, tiled=True)
        for part in select(demanded, tile_count, fields)
    ]
    local = jnp.mod(destination_block - server * band, band * servers)
    entry, rank = block_src % capacity, block_src // capacity
    n_rows = band + 1
    steps_max = -(-slots // UNIT) + capacity * n_rows
    starts, slot, src = plan(entry * n_rows + local, block_live == 1, capacity * n_rows, rank, steps_max)
    totals = products(starts, slot, src, received[0], weights, 0, n_rows)
    piece = jax.ShapeDtypeStruct((rows, width), jnp.float32)
    (excess,) = products(
        starts, slot, src, received[1], weights, n_rows + band, n_rows + n_rows, totals[band:], finish_excess, (piece,)
    )
    arrived = lax.ppermute(excess, "srv", [(i, (i + 1) % servers) for i in range(servers)])
    body = jax.ShapeDtypeStruct((band, rows, width), jnp.bfloat16)
    out, head = products(
        starts, slot, src, received[1], weights, n_rows, n_rows + band, totals[:band], finish_rows, (body, piece)
    )
    return out.at[0].set((head + arrived).astype(jnp.bfloat16))


def solution(mesh):
    in_specs = (
        P(("groups", "srv"), None, None),
        P("srv"),
        P("srv", None, None),
        P("srv", None, None),
        P("srv"),
        P("srv"),
        P("srv"),
    )
    out_specs = P(("groups", "srv"), None, None)
    return jax.shard_map(shards, mesh=mesh, in_specs=in_specs, out_specs=out_specs, check_vma=False)
```

time: 419 us -> 149 us (0.36); the launches traced: 412 us -> 149 us
  other arithmetic: 140 us -> 2.43 us
  matrix products: 109 us -> 0 us
  Pallas kernels: 0 us -> 76.6 us
  local copies, waits for them, and re-layouts: 85.5 us -> 17.7 us
  waiting for transfers between devices: 58.9 us -> 0.01 us
  blocking collectives: 0 us -> 47.7 us
  starting transfers between devices: 18 us -> 4.67 us
    scatter-add x19 -> x0, other arithmetic: 137 us -> none  [the longest x18 136 us: accumulate(): return (totals.at[rows_group].add(weighted_products), None)]
    dot_general x18 -> x0, matrix products: 109 us -> none  [accumulate(): jnp.einsum('krc,kdc->krd', received[source_group], w_group, preferred_ele...]
    gather x19 -> x0, local copies, waits for them, and re-layouts: 80 us -> none  [the longest x18 77.6 us: accumulate(): received[source_group]]
    pallas_call x0 -> x4, Pallas kernels: none -> 76.6 us  [the longest x3 74.4 us: products(): pl.pallas_call(functools.partial(product_kernel, first, last, finish), ou...]
    all_to_all x2 -> x1, waiting for transfers between devices: 57.8 us -> 0.01 us  [shards(): lax.all_to_all(part, 'srv', split_axis=0, concat_axis=0, tiled=True)]
    all_to_all x0 -> x2, blocking collectives: none -> 47.7 us  [the longest x1 36.6 us: shards(): lax.all_to_all(part, 'srv', split_axis=0, concat_axis=0, tiled=True)]
    unnamed x8 -> x16, local copies, waits for them, and re-layouts: 1.54 us -> 14.6 us
    all_to_all x2 -> x1, starting transfers between devices: 12.1 us -> 4.61 us  [shards(): lax.all_to_all(part, 'srv', split_axis=0, concat_axis=0, tiled=True)]
  transfers between devices with their start and end apart: 3 -> 2, of which waited for: 3 -> 0; matrix products, arithmetic and copies ran while one was open for 1% -> 2% of each run, Pallas kernels for 0% -> 48%
where the time goes in v1:
time: 149 us
  Pallas kernels  76.6 us (51%)
  blocking collectives  47.7 us (32%)
  local copies, waits for them, and re-layouts  17.7 us (12%)
  starting transfers between devices  4.67 us (3%)
  other arithmetic  2.43 us (2%)
    pallas_call x3, Pallas kernels, products(): pl.pallas_call(functools.partial(product_kernel, first, last, finish), ou...  74.4 us
    all_to_all x1, blocking collectives, shards(): lax.all_to_all(part, 'srv', split_axis=0, concat_axis=0, tiled=True)  36.6 us
    unnamed x16, local copies, waits for them, and re-layouts  14.6 us
    all_to_all x1, blocking collectives, shards(): lax.all_to_all(route[0], 'srv', split_axis=0, concat_axis=0, tiled=True)  11.1 us
    all_to_all x1, starting transfers between devices, shards(): lax.all_to_all(part, 'srv', split_axis=0, concat_axis=0, tiled=True)  4.61 us
  transfers between devices with their start and end apart: 2, of which 0 were waited for; matrix products, arithmetic and copies ran while one was open for 2% of the time, Pallas kernels for 48%

profile of v1, /device:TPU:7, one launch (start us, length us, event | category | flops | bytes accessed | tf_op | source)
XLA Modules:
  0.0 149.3 jit_solution(3349467461372963564)
XLA Ops:
  0.0 0.8 copy.11
  0.8 11.1 %all_to_all.19 = s32[16,1,2]{2,1,0:T(1,128)S(1)} all-to-all(s32[16,1,2]{2,1,0:T(1,128)S(1)} %copy.11), channel_id=1, replica_groups=mesh['groups'=2,'srv'=16] {'srv'}, dimensions={0} | all-to-all | bytes 256 | tf_op jit(solution)/shard_map/all_to_all | solution.py:171
  11.9 0.5 broadcast.97
  12.4 0.7 reduce.5
  13.1 0.1 reshape.64.demanded
  13.2 0.0 copy-start.3
  13.2 1.2 copy-done.3
  14.4 0.0 copy-start.4
  14.4 0.7 copy-done.4
  15.1 2.2 %shard_map.73 = (bf16[16,336,128]{2,1,0:T(8,128)(2,1)S(1)}, bf16[16,336,128]{2,1,0:T(8,128)(2,1)}) custom-call(s32[32]{0:T(128)S(1)} %reshape.64.demanded, s32[12]{0:T(128)S(1)} %copy-done.4, bf16[12,336,128]{2,1,0:T(8,128)(2,1)S(1)} %copy-done.3), custom_call_target="tpu_custom_call" | custom-call | tf_op jit(solution)/shard_map/pallas_call | solution.py:141
  17.2 36.6 %all_to_all.20.x_hbm = bf16[16,336,128]{2,1,0:T(8,128)(2,1)S(1)} all-to-all(bf16[16,336,128]{2,1,0:T(8,128)(2,1)S(1)} %get-tuple-element.22), channel_id=1, replica_groups=mesh['groups'=2,'srv'=16] {'srv'}, dimensions={0} | all-to-all | bytes 2752512 | tf_op jit(solution)/shard_map/all_to_all | solution.py:173
  53.8 4.6 %all-to-all-start.1 = ((bf16[16,336,128]{2,1,0:T(8,128)(2,1)}), bf16[16,336,128]{2,1,0:T(8,128)(2,1)S(1)}, u32[]{:S(2)}, u32[]{:S(2)}) async-start(bf16[16,336,128]{2,1,0:T(8,128)(2,1)} %get-tuple-element.21), calls=%async_computation.1 | async-start | bytes 2752512 | tf_op jit(solution)/shard_map/all_to_all | solution.py:173
  58.5 0.0 copy-done.5
  58.5 0.0 copy-done.6
  58.5 0.0 copy-done.7
  58.5 0.1 convert_reduce_fusion.1
  58.7 0.1 select_reduce_fusion.3.starts
  58.8 0.1 select_reduce_fusion.2
  58.9 0.3 convert_reduce_fusion
  59.2 0.4 select_reduce_fusion
  59.6 0.0 copy-start
  59.6 6.4 %copy-done = bf16[576,128,128]{2,1,0:T(8,128)(2,1)S(1)} copy-done((bf16[576,128,128]{2,1,0:T(8,128)(2,1)S(1)}, bf16[576,128,128]{2,1,0:T(8,128)(2,1)}, u32[]{:S(2)}) %copy-start) | copy-done | bytes 18874392
  66.0 32.5 %shard_map.74 = f32[17,336,128]{2,1,0:T(8,128)S(1)} custom-call(s32[35]{0:T(128)S(1)} %select_reduce_fusion.3.starts, s32[712]{0:T(1024)S(1)} %get-tuple-element.26.slot, s32[712]{0:T(1024)S(1)} %broadcast_add_fusion.src, bf16[16,336,128]{2,1,0:T(8,128)(2,1)S(1)} %all_to_all.20.x_hbm, bf16[576,128,128]{2,1,0:T(8,128)(2,1)S(1)} %copy-done), custom_call_target="tpu_custom_call" | custom-call | flops 6341787648 | bytes 18874368 | tf_op jit(solution)/shard_map/pallas_call | solution.py:103
  98.5 1.7 %slice.28.refs_0_ = f32[16,336,128]{2,1,0:T(8,128)} slice(f32[17,336,128]{2,1,0:T(8,128)S(1)} %shard_map.74), slice={[0:16], [0:336], [0:128]} | slice | bytes 5505024 | tf_op jit(solution)/shard_map/slice | solution.py:189
  100.3 0.0 all-to-all-done.1.x_hbm
  100.3 6.4 %copy-done.1 = bf16[576,128,128]{2,1,0:T(8,128)(2,1)S(1)} copy-done((bf16[576,128,128]{2,1,0:T(8,128)(2,1)S(1)}, bf16[576,128,128]{2,1,0:T(8,128)(2,1)}, u32[]{:S(2)}) %copy-start.1) | copy-done | bytes 18874392
  106.6 2.9 %shard_map.76 = f32[336,128]{1,0:T(8,128)S(1)} custom-call(s32[35]{0:T(128)S(1)} %select_reduce_fusion.3.starts, s32[712]{0:T(1024)S(1)} %get-tuple-element.26.slot, s32[712]{0:T(1024)S(1)} %broadcast_add_fusion.src, bf16[16,336,128]{2,1,0:T(8,128)(2,1)S(1)} %all-to-all-done.1.x_hbm, bf16[576,128,128]{2,1,0:T(8,128)(2,1)S(1)} %copy-done.1, ...), custom_call_target="tpu_custom_call" | custom-call | flops 352321536 | bytes 1048576 | tf_op jit(solution)/shard_map/pallas_call | solution.py:103
  109.5 0.1 collective-permute-start
  109.6 0.0 copy-done.2
  109.6 39.0 %shard_map.75 = (bf16[16,336,128]{2,1,0:T(8,128)(2,1)}, f32[336,128]{1,0:T(8,128)S(1)}) custom-call(s32[35]{0:T(128)S(1)} %select_reduce_fusion.3.starts, s32[712]{0:T(1024)S(1)} %get-tuple-element.26.slot, s32[712]{0:T(1024)S(1)} %broadcast_add_fusion.src, bf16[16,336,128]{2,1,0:T(8,128)(2,1)S(1)} %all-to-all-done.1.x_hbm, ...), custom_call_target="tpu_custom_call" | custom-call | flops 5967446016 | bytes 17760256 | tf_op jit(solution)/shard_map/pallas_call | solution.py:103
  148.7 0.0 collective-permute-done
  148.7 0.7 fusion.3
  (11 shorter events, 0.1 us)
Async XLA Ops:
  13.2 1.2 copy-start.3
  14.4 0.7 copy-start.4
  53.8 4.6 %copy-start.5 = (s32[576]{0:T(1024)S(1)}, s32[576]{0:T(1024)}, u32[]{:S(2)}) copy-start(s32[576]{0:T(1024)} %param.15) | copy-start | bytes 6916
  53.8 4.6 %copy-start.6 = (s32[576]{0:T(1024)S(1)}, s32[576]{0:T(1024)}, u32[]{:S(2)}) copy-start(s32[576]{0:T(1024)} %param.13) | copy-start | bytes 6916
  53.8 4.6 %copy-start.7 = (s32[576]{0:T(1024)S(1)}, s32[576]{0:T(1024)}, u32[]{:S(2)}) copy-start(s32[576]{0:T(1024)} %param.14) | copy-start | bytes 6916
  53.8 46.4 %all-to-all-start.1 = ((bf16[16,336,128]{2,1,0:T(8,128)(2,1)}), bf16[16,336,128]{2,1,0:T(8,128)(2,1)S(1)}, u32[]{:S(2)}, u32[]{:S(2)}) async-start(bf16[16,336,128]{2,1,0:T(8,128)(2,1)} %get-tuple-element.21), calls=%async_computation.1 | async-start | bytes 2752512 | tf_op jit(solution)/shard_map/all_to_all | solution.py:173
  59.6 6.4 %copy-start = (bf16[576,128,128]{2,1,0:T(8,128)(2,1)S(1)}, bf16[576,128,128]{2,1,0:T(8,128)(2,1)}, u32[]{:S(2)}) copy-start(bf16[576,128,128]{2,1,0:T(8,128)(2,1)} %w_hbm.5) | copy-start | bytes 56623108
  100.3 6.4 %copy-start.1 = (bf16[576,128,128]{2,1,0:T(8,128)(2,1)S(1)}, bf16[576,128,128]{2,1,0:T(8,128)(2,1)}, u32[]{:S(2)}) copy-start(bf16[576,128,128]{2,1,0:T(8,128)(2,1)} %w_hbm.5) | copy-start | bytes 56623108
  106.6 3.0 %copy-start.2 = (f32[16,336,128]{2,1,0:T(8,128)S(1)}, f32[16,336,128]{2,1,0:T(8,128)}, u32[]{:S(2)}) copy-start(f32[16,336,128]{2,1,0:T(8,128)} %slice.28.refs_0_) | copy-start | bytes 8257540
  109.5 39.1 %collective-permute-start = (f32[336,128]{1,0:T(8,128)S(1)}, f32[336,128]{1,0:T(8,128)S(1)}, u32[]{:S(2)}, u32[]{:S(2)}) collective-permute-start(f32[336,128]{1,0:T(8,128)S(1)} %shard_map.76), channel_id=1, source_target_pairs={{0,1},{1,2},{2,3},{3,4},{4,5},{5,6},{6,7},{7,8},{8,9},{9,10},{10,1... | collective-permute-start | bytes 516104 | tf_op jit(solution)/shard_map/ppermute | solution.py:186
